TPU v7x, 256 devices: a whole 4x4x8 slice. The times are simulated.
256 devices in a mesh: dp: 64 (over x, y, z_hi), tensor: 4 (over z_lo, core).
Axes of the slice: x: 4, y: 4, z: 8 (z_hi: 4, z_lo: 2; z = z_hi * 2 + z_lo), core: 2. Of those that a mesh axis runs over, the one named last changes fastest.
Arguments:
- hidden: bfloat16 [128, 256, 4096], P('dp', None, 'tensor'), may hold values from -6 to 6
- targets: int32 [128, 256], P('dp'), may hold values from 0 to 511
- lengths: int32 [128], P('dp'), may hold values from 1 to 256, 16384 in all
- conv_filter: bfloat16 [3, 4096], P(None, 'tensor'), may hold values from -3 to 3
- proj_weight: bfloat16 [4096, 4096], P('tensor'), may hold values from -0.09375 to 0.09375
- unembed: bfloat16 [512, 4096], P(None, 'tensor'), may hold values from -0.140625 to 0.140625
- proj_in: bfloat16 [4096, 64], P('tensor'), may hold values from -0.09375 to 0.09375
- proj_out: bfloat16 [4096, 64], P('tensor'), may hold values from -0.09375 to 0.09375
- query_grads: bfloat16 [1024, 4096], P('dp', 'tensor'), may hold values from -6 to 6
Outputs:
- scores: float32 [128, 1024], P('dp')
Inputs may be any that keep to these rules, and one draw needn't show every extreme that they name: `lengths`: some row has exactly 256 live tokens.
All inputs are finite; a program needn't handle non-finite values. No bound on the sum of `lengths` on one device may be relied on, other than what follows from the above.
Results may differ from a plain program's by a relative error of at most 0.0075.
Values may be sent and summed in bfloat16 or wider, within the bound.
A program may use at most 64 MiB of HBM per device.

v0:
```python
import jax
import jax.numpy as jnp
from jax import lax
from jax.sharding import PartitionSpec as P

eps = 1e-06


def short_conv(hidden, conv_filter):
    values = hidden.astype(jnp.float32)
    taps = conv_filter.astype(jnp.float32)
    zero = jnp.zeros_like(values[..., :1, :])
    first = jnp.concatenate([zero, values[..., :-1, :]], axis=-2)
    second = jnp.concatenate([zero, zero, values[..., :-2, :]], axis=-2)
    return (taps[0] * values + taps[1] * first + taps[2] * second).astype(jnp.bfloat16)


def per_device(
    hidden, targets, lengths, conv_filter, proj_weight, unembed, proj_in, proj_out, query_grads
):
    rows, length, local_width = hidden.shape
    tokens = rows * length
    rank = proj_in.shape[1]
    vocab = unembed.shape[0]
    mixed = short_conv(hidden, conv_filter).reshape(tokens, local_width)
    layer_out = lax.psum_scatter(
        lax.dot_general(
            proj_weight, mixed, (((0,), (1,)), ((), ())), preferred_element_type=jnp.float32
        ),
        "tensor",
        scatter_dimension=0,
        tiled=True,
    )
    layer_low = layer_out.astype(jnp.bfloat16)
    partial_logits = jnp.dot(unembed, layer_low, preferred_element_type=jnp.float32)
    logits = lax.psum(partial_logits, "tensor")
    expo = jnp.exp(logits)
    prob = expo / jnp.sum(expo, axis=0, keepdims=True)
    live = (jnp.arange(length)[None, :] < lengths[:, None]).astype(jnp.float32).reshape(tokens)
    onehot = (jnp.arange(vocab)[:, None] == targets.reshape(tokens)[None, :]).astype(jnp.float32)
    grad_logits = ((prob - onehot) * live[None, :]).astype(jnp.bfloat16)
    grad_out = lax.dot_general(
        unembed, grad_logits, (((0,), (0,)), ((), ())), preferred_element_type=jnp.float32
    ).astype(jnp.bfloat16)
    part_in = lax.dot_general(
        proj_in, mixed, (((0,), (1,)), ((), ())), preferred_element_type=jnp.float32
    )
    part_out = lax.dot_general(
        proj_out, grad_out, (((0,), (0,)), ((), ())), preferred_element_type=jnp.float32
    )
    share = rank // lax.axis_size("tensor")
    whole_in, whole_out = lax.psum((part_in, part_out), "tensor")
    share_in = lax.dynamic_slice_in_dim(whole_in, lax.axis_index("tensor") * share, share, 0)
    row_grad = jnp.einsum(
        "irt,jrt->rij",
        share_in.reshape(share, rows, length),
        whole_out.reshape(rank, rows, length),
        precision=lax.Precision.HIGHEST,
    )
    row_grad = row_grad.reshape(rows, share * rank)
    row_norm = jnp.sum(row_grad * row_grad, axis=1)
    row_low = row_grad.astype(jnp.bfloat16)
    partial_scores = lax.dot_general(
        row_low,
        lax.all_gather(query_grads, "dp", axis=0, tiled=True),
        (((1,), (1,)), ((), ())),
        preferred_element_type=jnp.float32,
    )
    inner, norms = lax.psum((partial_scores, row_norm), "tensor")
    return inner / jnp.sqrt(norms + eps)[:, None]


def solution(mesh):
    in_specs = (
        P("dp", None, "tensor"),
        P("dp", None),
        P("dp"),
        P(None, "tensor"),
        P("tensor", None),
        P(None, "tensor"),
        P("tensor", None),
        P("tensor", None),
        P("dp", "tensor"),
    )
    out_specs = P("dp", None)
    return jax.shard_map(
        per_device, mesh=mesh, in_specs=in_specs, out_specs=out_specs, check_vma=False
    )
```

profile of v0, /device:TPU:1, one launch (start us, length us, event | category | flops | bytes accessed | tf_op | source)
XLA Modules:
  0.0 258.6 jit_solution(10185630679058435989)
XLA Ops:
  7.4 1.6 slice.22
  9.0 0.2 slice.24
  9.3 0.4 copy-done.3
  9.7 0.8 add_convert_fusion
  10.5 1.9 copy-done.6
  12.4 6.7 %convolution_bitcast_fusion = f32[4096,512]{0,1:T(8,128)} fusion(bf16[512,1024]{1,0:T(8,128)(2,1)S(1)} %bitcast.36, bf16[1024,4096]{1,0:T(8,128)(2,1)S(1)} %copy-done.6), kind=kOutput, calls=%fused_computation | convolution fusion | flops 4294967296 | bytes 17825792 | tf_op jit(solution)/shard_map/dot_general | solution.py:27
  19.2 85.8 %reduce-scatter.2.cloned.1.call-done = f32[1024,512]{0,1:T(8,128)} async-done(((f32[4096,512]{0,1:T(8,128)}), f32[1024,512]{0,1:T(8,128)}) %reduce-scatter.2.cloned.1.call-update) | async-done | bytes 2097168 | tf_op jit(solution)/shard_map/reduce_scatter | solution.py:26
  105.0 3.3 %convolution_bitcast_fusion.1 = f32[512,512]{0,1:T(8,128)} fusion(bf16[512,1024]{1,0:T(8,128)(2,1)S(1)} %copy-done, f32[1024,512]{0,1:T(8,128)} %reduce-scatter.2.cloned.1.call-done), kind=kOutput, calls=%fused_computation.4 | convolution fusion | flops 537395200 | bytes 4194304 | tf_op jit(solution)/shard_map/dot_general | solution.py:35
  108.4 0.1 fusion.11
  108.5 1.1 convolution_bitcast_fusion.2
  109.6 45.4 %all-reduce.7.cloned.1.call-done = f32[512,512]{0,1:T(8,128)} async-done(((f32[512,512]{0,1:T(8,128)}), f32[512,512]{0,1:T(8,128)}) %all-reduce.7.cloned.1.call-update) | async-done | bytes 1048592 | tf_op jit(solution)/shard_map/psum | solution.py:36
  155.0 1.4 exponential_reduce_fusion
  156.5 2.4 fusion
  158.8 0.7 copy.24
  159.5 0.0 all-gather.2.cloned.1.call-start
  159.6 0.5 all-gather.2.cloned.1.call-update
  160.1 41.5 %all-reduce.9.cloned.1.call-done = (f32[64,2,256]{2,0,1:T(8,128)}, f32[64,512]{1,0:T(8,128)}) async-done(((f32[64,2,256]{2,0,1:T(8,128)}, f32[64,512]{1,0:T(8,128)}), (f32[64,2,256]{2,0,1:T(8,128)}, f32[64,512]{1,0:T(8,128)})) %all-reduce.9.cloned.1.call-update) | async-done | bytes 262160 | tf_op jit(solution)/shard_map/psum | solution.py:52
  201.6 0.8 constant_dynamic-slice_fusion
  202.4 1.2 multiply_reduce_fusion
  203.6 0.1 convert_element_type.48
  203.7 36.4 %all-gather.2.cloned.1.call-done = bf16[1024,1024]{1,0:T(8,128)(2,1)} async-done(((bf16[16,1024]{1,0:T(8,128)(2,1)}), bf16[1024,1024]{1,0:T(8,128)(2,1)}) %all-gather.2.cloned.1.call-update) | async-done | bytes 2097168 | tf_op jit(solution)/shard_map/all_gather | solution.py:65
  240.1 2.2 fusion.13
  242.3 8.5 %all-reduce.2 = (f32[2,1024]{1,0:T(2,128)S(1)}, f32[2]{0:T(128)S(1)}) all-reduce(f32[2,1024]{1,0:T(2,128)S(1)} %fusion.13, f32[2]{0:T(128)S(1)} %get-tuple-element.9), channel_id=1, replica_groups=mesh['dp'=64,'tensor'=4] {'tensor'}, use_global_device_ids=true, to_apply=%region_5.0 | all-reduce | flops 2050 | bytes 16400 | tf_op jit(solution)/shard_map/psum | solution.py:69
  250.8 0.7 broadcast_divide_fusion
  (24 shorter events, 0.2 us)
Async XLA Ops:
  7.4 97.7 %copy-start = (bf16[512,1024]{1,0:T(8,128)(2,1)S(1)}, bf16[512,1024]{1,0:T(8,128)(2,1)}, u32[]{:S(2)}) copy-start(bf16[512,1024]{1,0:T(8,128)(2,1)} %param.14) | copy-start | bytes 3145732
  7.4 97.7 %reduce-scatter.2.cloned.1.call-start = ((), (), s32[]{:S(2)}) async-start(), calls=%async_computation.1 | async-start | bytes 10485760 | tf_op jit(solution)/shard_map/reduce_scatter | solution.py:26
  7.4 1.6 copy-start.1
  9.0 0.7 copy-start.3
  9.0 3.4 %copy-start.6 = (bf16[1024,4096]{1,0:T(8,128)(2,1)S(1)}, bf16[1024,4096]{1,0:T(8,128)(2,1)}, u32[]{:S(2)}) copy-start(bf16[1024,4096]{1,0:T(8,128)(2,1)} %param.13) | copy-start | bytes 25165828
  19.1 89.3 %copy-start.5 = (s32[2]{0:T(128)S(1)}, s32[2]{0:T(128)}, u32[]{:S(2)}) copy-start(s32[2]{0:T(128)} %param.11) | copy-start | bytes 28
  19.2 89.3 %copy-start.4 = (s32[2,256]{1,0:T(2,128)S(1)}, s32[2,256]{1,0:T(2,128)}, u32[]{:S(2)}) copy-start(s32[2,256]{1,0:T(2,128)} %param.10) | copy-start | bytes 6148
  19.2 89.3 %copy-start.2 = (bf16[1024,64]{0,1:T(8,128)(2,1)S(1)}, bf16[1024,64]{0,1:T(8,128)(2,1)}, u32[]{:S(2)}) copy-start(bf16[1024,64]{0,1:T(8,128)(2,1)} %param.15) | copy-start | bytes 393220
  19.2 135.8 %all-reduce.7.cloned.1.call-start = ((), (), s32[]{:S(2)}) async-start(), calls=%async_computation.2 | async-start | bytes 2097152 | tf_op jit(solution)/shard_map/psum | solution.py:36
  108.3 48.1 %copy-start.7 = (bf16[1024,64]{0,1:T(8,128)(2,1)S(1)}, bf16[1024,64]{0,1:T(8,128)(2,1)}, u32[]{:S(2)}) copy-start(bf16[1024,64]{0,1:T(8,128)(2,1)} %param.16) | copy-start | bytes 393220
  108.4 93.2 %all-reduce.9.cloned.1.call-start = ((), (), s32[]{:S(2)}) async-start(), calls=%async_computation.4 | async-start | bytes 524288 | tf_op jit(solution)/shard_map/psum | solution.py:52
  159.5 80.5 %all-gather.2.cloned.1.call-start = ((), (), s32[]{:S(2)}) async-start(), calls=%async_computation.3 | async-start | bytes 2129920 | tf_op jit(solution)/shard_map/all_gather | solution.py:65
Sparse Core Ops, SparseCore 0:
  19.3 85.7 reduce-scatter.1
  108.5 46.5 all-reduce.6
  159.7 41.9 all-reduce.8
Sparse Core Ops, SparseCore 1:
  163.3 76.7 all-gather.1
where the time goes:
time: 259 us
  waiting for transfers between devices  210 us (81%)
  matrix products  16.9 us (7%)
  between operations  14.7 us (6%)
  blocking collectives  8.45 us (3%)
  local copies, waits for them, and re-layouts  5.76 us (2%)
  other arithmetic  2.97 us (1%)
    reduce_scatter x1, waiting for transfers between devices, per_device(): lax.psum_scatter(lax.dot_general(proj_weight, mixed, (((0,), (1,)), ((),...  85.8 us
    psum x1, waiting for transfers between devices, per_device(): logits = lax.psum(partial_logits, 'tensor')  45.4 us
    psum x1, waiting for transfers between devices, per_device(): whole_in, whole_out = lax.psum((part_in, part_out), 'tensor')  41.5 us
    all_gather x1, waiting for transfers between devices, per_device(): lax.all_gather(query_grads, 'dp', axis=0, tiled=True)  36.4 us
    psum x1, blocking collectives, per_device(): inner, norms = lax.psum((partial_scores, row_norm), 'tensor')  8.45 us
    dot_general x1, matrix products, per_device(): lax.dot_general(proj_weight, mixed, (((0,), (1,)), ((), ())), preferred_e...  6.72 us
  transfers between devices with their start and end apart: 4, of which 4 were waited for; matrix products, arithmetic and copies ran while one was open for 1% of the time, Pallas kernels for 0%

commit v1 on v0

v1 whole, which is shorter than its diff:
```python
import functools

import jax
import jax.numpy as jnp
from jax import lax
from jax.experimental import pallas as pl
from jax.experimental.pallas import tpu as pltpu
from jax.sharding import PartitionSpec as P

EPS = 1e-06
MESH = pl.DeviceIdType.MESH
F32 = jnp.float32
BF16 = jnp.bfloat16

LOCAL = 512
WIDTH = 1024
SIDE = 64
ROWS = LOCAL + SIDE
BLOCKS = 4
BLOCK = LOCAL // BLOCKS
HALF = BLOCK // 2


def nt(left, right, precision=None):
    return lax.dot_general(
        left, right, (((1,), (1,)), ((), ())), precision=precision, preferred_element_type=F32
    )


def kernel(
    hidden,
    targets,
    lengths,
    conv_filter,
    proj_weight,
    unembed,
    proj_in_t,
    proj_out_t,
    queries,
    out,
    held,
    mixed,
    weight,
    words,
    side_in_w,
    side_out_w,
    folded,
    folded_low,
    up_part,
    up_sib,
    up_chip,
    up_far,
    logits_full,
    logits_low,
    from_sib,
    to_far,
    from_far,
    side_t,
    query_all,
    grad_out,
    grad_all,
    grad_rows,
    score_out,
    score_all,
    local_sem,
    uz_send,
    uz_recv,
    us_send,
    us_recv,
    uf_send,
    uf_recv,
    up_send,
    up_recv,
    a_send,
    a_recv,
    b_send,
    b_recv,
    q_send,
    q_recv,
    g_send,
    g_recv,
    s_send,
    s_recv,
):
    dp = lax.axis_index("dp")
    tensor = lax.axis_index("tensor")
    plane, zh = dp // 4, dp % 4
    zl, core = tensor // 2, tensor % 2
    me = zh * 4 + tensor
    sib = (dp, zl * 2 + 1 - core)
    near = (dp, (1 - zl) * 2 + core)
    far = (plane * 4 + (zh + 2 * zl + 3) % 4, (1 - zl) * 2 + core)

    def column(place):
        return (plane * 4 + place // 4, place % 4)

    def in_plane(place):
        return (place * 4 + zh, tensor)

    def remote(src, dst, send, recv, device):
        return pltpu.make_async_remote_copy(
            src_ref=src, dst_ref=dst, send_sem=send, recv_sem=recv, device_id=device, device_id_type=MESH
        )

    barrier = pltpu.get_barrier_semaphore()
    for step in range(1, 16):
        pl.semaphore_signal(barrier, inc=1, device_id=column((me + step) % 16), device_id_type=MESH)
        pl.semaphore_signal(barrier, inc=1, device_id=in_plane((plane + step) % 16), device_id_type=MESH)

    own_slices = (tensor, zl * 2 + 1 - core, (1 - zl) * 2 + core, (1 - zl) * 2 + 1 - core)
    loads = [
        pltpu.make_async_copy(hidden, held, local_sem.at[0]),
        pltpu.make_async_copy(unembed, words.at[0], local_sem.at[1]),
        pltpu.make_async_copy(proj_out_t, side_out_w, local_sem.at[2]),
        pltpu.make_async_copy(proj_in_t, side_in_w, local_sem.at[3]),
    ] + [
        pltpu.make_async_copy(
            proj_weight.at[:, pl.ds(pl.multiple_of(own_slices[i] * WIDTH, WIDTH), WIDTH)],
            weight.at[i],
            local_sem.at[4 + i],
        )
        for i in range(4)
    ] + [
        pltpu.make_async_copy(
            queries, query_all.at[pl.ds(pl.multiple_of(plane * 16, 16), 16)], local_sem.at[8]
        )
    ]
    for load in loads:
        load.start()

    pl.semaphore_wait(barrier, 30)

    sends = []
    to_sib = remote(unembed, words.at[1], us_send, us_recv, sib)
    word_copies = []
    for b in range(BLOCKS):
        pair = []
        for side, device in enumerate((near, far)):
            rows = pl.ds(b * BLOCK + side * HALF, HALF)
            copy = remote(
                unembed.at[rows], words.at[2, rows], uz_send.at[b, side], uz_recv.at[b, side], device
            )
            copy.start()
            pair.append(copy)
        word_copies.append(pair)
        sends.extend(pair)
        if b == 0:
            to_sib.start()
    sends.append(to_sib)

    query_copies = []
    for step in range(1, 16):
        copy = remote(
            queries,
            query_all.at[pl.ds(pl.multiple_of(plane * 16, 16), 16)],
            q_send.at[step],
            q_recv.at[step],
            in_plane((plane + step) % 16),
        )
        copy.start()
        query_copies.append(copy)
    sends.extend(query_copies)

    loads[0].wait()
    chunk = 256
    first_row = lax.broadcasted_iota(jnp.int32, (256, chunk), 0)

    def convolve(i, carry):
        row = i // (WIDTH // chunk)
        columns = pl.ds(pl.multiple_of((i % (WIDTH // chunk)) * chunk, chunk), chunk)
        values = held[row, :, columns].astype(F32)
        taps = conv_filter[:, columns].astype(F32)
        first = jnp.where(first_row < 1, 0.0, pltpu.roll(values, 1, 0))
        second = jnp.where(first_row < 2, 0.0, pltpu.roll(values, 2, 0))
        result = taps[0:1] * values + taps[1:2] * first + taps[2:3] * second
        mixed[pl.ds(pl.multiple_of(row * 256, 256), 256), columns] = result.astype(BF16)
        return carry

    lax.fori_loop(0, 2 * (WIDTH // chunk), convolve, 0)

    loads[1].wait()
    loads[2].wait()
    up_part[...] = nt(side_out_w[...], words[0])
    up_to_sib = remote(up_part, up_sib, up_send.at[0], up_recv.at[0], sib)
    up_to_sib.start()
    sends.append(up_to_sib)

    loads[4].wait()
    folded[...] = nt(words[0], weight[0])

    loads[3].wait()

    def put(rows, part):
        for quarter in range(4):
            logits_full[quarter % 2, quarter // 2, rows] = part[:, quarter * 128 : (quarter + 1) * 128]
            logits_low[quarter % 2, quarter // 2, rows] = part[:, quarter * 128 : (quarter + 1) * 128].astype(
                BF16
            )

    def send_a(index, rows):
        copy = remote(
            logits_low.at[1 - core, :, rows], from_sib.at[:, rows], a_send.at[index], a_recv.at[index], sib
        )
        copy.start()
        sends.append(copy)
        return copy

    def send_b(index, rows, copy):
        copy.wait_recv()
        chip = logits_full[core, 1 - zl, rows] + from_sib[1 - zl, rows].astype(F32)
        to_far[rows] = chip.astype(BF16)
        result = remote(to_far.at[rows], from_far.at[rows], b_send.at[index], b_recv.at[index], near)
        result.start()
        sends.append(result)
        return result

    side_rows = pl.ds(LOCAL, SIDE)
    put(side_rows, nt(side_in_w[...], mixed[...]))
    side_a = send_a(BLOCKS, side_rows)

    up_to_sib.wait_recv()
    up_chip[...] = up_part[...] + up_sib[...]
    up_copies = []
    for side, device in enumerate((near, far)):
        rows = pl.ds(side * (SIDE // 2), SIDE // 2)
        copy = remote(up_chip.at[rows], up_far.at[rows], up_send.at[1 + side], up_recv.at[1 + side], device)
        copy.start()
        up_copies.append(copy)
    sends.extend(up_copies)

    to_sib.wait_recv()
    loads[5].wait()
    folded[...] += nt(words[1], weight[1])
    b_copies = [send_b(BLOCKS, side_rows, side_a)]

    loads[6].wait()
    loads[7].wait()
    previous = None
    for b in range(BLOCKS):
        rows = pl.ds(b * BLOCK, BLOCK)
        for copy in word_copies[b]:
            copy.wait_recv()
        forward = remote(words.at[2, rows], words.at[3, rows], uf_send.at[b], uf_recv.at[b], sib)
        forward.start()
        sends.append(forward)
        part = folded[rows] + nt(words[2, rows], weight[2])
        if previous is not None:
            b_copies.append(send_b(*previous))
        forward.wait_recv()
        folded_low[rows] = (part + nt(words[3, rows], weight[3])).astype(BF16)
        put(rows, nt(folded_low[rows], mixed[...]))
        previous = (b, rows, send_a(b, rows))
    b_copies.append(send_b(*previous))

    for copy in up_copies:
        copy.wait_recv()
    up = (up_chip[...] + up_far[...]).astype(BF16)
    for copy in b_copies:
        copy.wait_recv()
    total = logits_full[core, zl] + from_sib[zl].astype(F32) + from_far[...].astype(F32)
    expo = jnp.exp(total[:LOCAL])
    prob = expo / jnp.sum(expo, axis=0, keepdims=True)
    place = lax.broadcasted_iota(jnp.int32, (1, 128), 1) + core * 128
    live = (place < lengths[zl]).astype(F32)
    ids = [jnp.where(zl == 0, targets[0:1, i : i + 128], targets[1:2, i : i + 128]) for i in (0, 128)]
    target = jnp.where(core == 0, ids[0], ids[1])
    onehot = (lax.broadcasted_iota(jnp.int32, (LOCAL, 128), 0) == target).astype(F32)
    grad_logits = ((prob - onehot) * live).astype(BF16)
    side_out = jnp.dot(up, grad_logits, preferred_element_type=F32)
    side_t[...] = total[LOCAL:]
    even = nt(side_t[pl.ds(0, SIDE // 2, stride=2), :], side_out, lax.Precision.HIGHEST)
    odd = nt(side_t[pl.ds(1, SIDE // 2, stride=2), :], side_out, lax.Precision.HIGHEST)
    row_grad = jnp.concatenate([even, odd], axis=1)
    for share in range(4):
        grad_out[share] = row_grad[share * 8 : (share + 1) * 8]

    grad_all[me] = grad_out[tensor]
    grad_copies = []
    for step in range(1, 16):
        place = (me + step) % 16
        copy = remote(grad_out.at[place % 4], grad_all.at[me], g_send.at[step], g_recv.at[step], column(place))
        copy.start()
        grad_copies.append(copy)
    sends.extend(grad_copies)
    for copy in query_copies:
        copy.wait_recv()
    loads[8].wait()
    for copy in grad_copies:
        copy.wait_recv()

    norms = []
    for row in range(8):
        whole = grad_all[2 * row] + grad_all[2 * row + 1]
        grad_rows[pl.ds(row * 8, 8)] = whole
        norms.append(jnp.sum(whole * whole, axis=(0, 1), keepdims=True))
    flat = jnp.concatenate([grad_rows[pl.ds(i, 8, stride=8), :] for i in range(8)], axis=1).astype(BF16)
    scores = nt(flat, query_all[...])
    for row in range(8):
        for half in range(2):
            score_out[row // 2, pl.ds((row % 2) * 2 + half, 1)] = scores[
                row : row + 1, half * 128 : (half + 1) * 128
            ]
            score_out[row // 2, pl.ds(4 + (row % 2) * 2 + half, 1)] = jnp.broadcast_to(norms[row], (1, 128))

    score_all[me] = score_out[zh]
    score_copies = []
    for step in range(1, 16):
        place = (me + step) % 16
        copy = remote(score_out.at[place // 4], score_all.at[me], s_send.at[step], s_recv.at[step], column(place))
        copy.start()
        score_copies.append(copy)
    sends.extend(score_copies)
    for copy in score_copies:
        copy.wait_recv()

    sums = [score_all[4 * i] + score_all[4 * i + 1] + score_all[4 * i + 2] + score_all[4 * i + 3] for i in range(4)]
    scale = jnp.sqrt(sums[0][4:8] + EPS)
    lane = lax.broadcasted_iota(jnp.int32, (8, 128), 1)
    for k in range(4):
        line = jnp.zeros((8, 128), F32)
        for i in range(4):
            for odd_one in range(2):
                source = 32 * k + 16 * odd_one
                target_lane = 64 * odd_one + 16 * i
                shift = (target_lane - source) % 128
                moved = pltpu.roll(sums[i], shift, 1) if shift else sums[i]
                line = jnp.where((lane >= target_lane) & (lane < target_lane + 16), moved, line)
        line = line[0:4] / scale
        for row in range(2):
            for half in range(2):
                out[pl.ds(row, 1), pl.ds(128 * (4 * half + k), 128)] = line[2 * row + half : 2 * row + half + 1]

    for copy in sends:
        copy.wait_send()


def per_device(hidden, targets, lengths, conv_filter, proj_weight, unembed, proj_in, proj_out, query_grads):
    hbm = pl.BlockSpec(memory_space=pltpu.HBM)
    vmem = pl.BlockSpec(memory_space=pltpu.VMEM)
    smem = pl.BlockSpec(memory_space=pltpu.SMEM)
    dma = pltpu.SemaphoreType.DMA
    scratch = [
        pltpu.VMEM((2, 256, WIDTH), BF16),
        pltpu.VMEM((LOCAL, WIDTH), BF16),
        pltpu.VMEM((4, WIDTH, WIDTH), BF16),
        pltpu.VMEM((4, LOCAL, WIDTH), BF16),
        pltpu.VMEM((SIDE, WIDTH), BF16),
        pltpu.VMEM((SIDE, WIDTH), BF16),
        pltpu.VMEM((LOCAL, WIDTH), F32),
        pltpu.VMEM((LOCAL, WIDTH), BF16),
        pltpu.VMEM((SIDE, LOCAL), F32),
        pltpu.VMEM((SIDE, LOCAL), F32),
        pltpu.VMEM((SIDE, LOCAL), F32),
        pltpu.VMEM((SIDE, LOCAL), F32),
        pltpu.VMEM((2, 2, ROWS, 128), F32),
        pltpu.VMEM((2, 2, ROWS, 128), BF16),
        pltpu.VMEM((2, ROWS, 128), BF16),
        pltpu.VMEM((ROWS, 128), BF16),
        pltpu.VMEM((ROWS, 128), BF16),
        pltpu.VMEM((SIDE, 128), F32),
        pltpu.VMEM((256, WIDTH), BF16),
        pltpu.VMEM((4, 8, 128), F32),
        pltpu.VMEM((16, 8, 128), F32),
        pltpu.VMEM((64, 128), F32),
        pltpu.VMEM((4, 8, 128), F32),
        pltpu.VMEM((16, 8, 128), F32),
        dma((9,)),
        dma((BLOCKS, 2)),
        dma((BLOCKS, 2)),
        dma,
        dma,
        dma((BLOCKS,)),
        dma((BLOCKS,)),
        dma((3,)),
        dma((3,)),
        dma((BLOCKS + 1,)),
        dma((BLOCKS + 1,)),
        dma((BLOCKS + 1,)),
        dma((BLOCKS + 1,)),
        dma((16,)),
        dma((16,)),
        dma((16,)),
        dma((16,)),
        dma((16,)),
        dma((16,)),
    ]
    return pl.pallas_call(
        kernel,
        out_shape=jax.ShapeDtypeStruct((2, 1024), F32),
        in_specs=[hbm, vmem, smem, vmem, hbm, hbm, hbm, hbm, hbm],
        out_specs=vmem,
        scratch_shapes=scratch,
        compiler_params=pltpu.CompilerParams(
            collective_id=0, has_side_effects=True, vmem_limit_bytes=48 * 1024 * 1024
        ),
        name="attribution",
    )(hidden, targets, lengths, conv_filter, proj_weight, unembed, proj_in.T, proj_out.T, query_grads)


def solution(mesh):
    in_specs = (
        P("dp", None, "tensor"),
        P("dp", None),
        P("dp"),
        P(None, "tensor"),
        P("tensor", None),
        P(None, "tensor"),
        P("tensor", None),
        P("tensor", None),
        P("dp", "tensor"),
    )
    return jax.shard_map(
        per_device, mesh=mesh, in_specs=in_specs, out_specs=P("dp", None), check_vma=False
    )
```

time: 259 us -> 51.9 us (0.20)
  waiting for transfers between devices: 210 us -> 0 us
  Pallas kernels: 0 us -> 43.9 us
  matrix products: 16.9 us -> 0 us
  between operations: 14.7 us -> 0.02 us
  blocking collectives: 8.45 us -> 0 us
  other arithmetic: 2.97 us -> 0 us
    psum x2 -> x0, waiting for transfers between devices: 86.9 us -> none  [the longest x1 45.4 us: per_device(): logits = lax.psum(partial_logits, 'tensor')]
    reduce_scatter x1 -> x0, waiting for transfers between devices: 85.8 us -> none  [per_device(): lax.psum_scatter(lax.dot_general(proj_weight, mixed, (((0,), (1,)), ((),...]
    pallas_call x0 -> x1, Pallas kernels: none -> 43.9 us  [per_device(): pl.pallas_call(kernel, out_shape=jax.ShapeDtypeStruct((2, 1024), F32), in...]
    all_gather x1 -> x0, waiting for transfers between devices: 36.4 us -> none  [per_device(): lax.all_gather(query_grads, 'dp', axis=0, tiled=True)]
    dot_general x6 -> x0, matrix products: 16.9 us -> none  [the longest x1 6.72 us: per_device(): lax.dot_general(proj_weight, mixed, (((0,), (1,)), ((), ())), preferred_e...]
    psum x1 -> x0, blocking collectives: 8.45 us -> none  [per_device(): inner, norms = lax.psum((partial_scores, row_norm), 'tensor')]
    unnamed x18 -> x17, local copies, waits for them, and re-layouts: 2.41 us -> 7.65 us
  transfers between devices with their start and end apart: 4 -> 0, of which waited for: 4 -> 0; matrix products, arithmetic and copies ran while one was open for 1% -> 0% of each run, Pallas kernels for 0% -> 0%
where the time goes in v1:
time: 51.9 us; the launch traced here: 51.6 us
  Pallas kernels  43.9 us (85%)
  local copies, waits for them, and re-layouts  7.65 us (15%)
    pallas_call x1, Pallas kernels, per_device(): pl.pallas_call(kernel, out_shape=jax.ShapeDtypeStruct((2, 1024), F32), in...  43.9 us
    unnamed x17, local copies, waits for them, and re-layouts  7.65 us

profile of v1, /device:TPU:1, one launch (start us, length us, event | category | flops | bytes accessed | tf_op | source)
XLA Modules:
  0.0 51.6 jit_solution(925353529164075224)
XLA Ops:
  0.0 0.0 copy-start
  0.0 1.2 %copy-done = bf16[2,256,1024]{2,1,0:T(8,128)(2,1)S(1)} copy-done((bf16[2,256,1024]{2,1,0:T(8,128)(2,1)S(1)}, bf16[2,256,1024]{2,1,0:T(8,128)(2,1)}, u32[]{:S(2)}) %copy-start) | copy-done | bytes 1048600
  1.2 0.0 copy-start.1
  1.2 1.2 %copy-done.1 = bf16[512,1024]{1,0:T(8,128)(2,1)S(1)} copy-done((bf16[512,1024]{1,0:T(8,128)(2,1)S(1)}, bf16[512,1024]{1,0:T(8,128)(2,1)}, u32[]{:S(2)}) %copy-start.1) | copy-done | bytes 1048600
  2.5 0.0 copy-start.2
  2.5 0.9 %copy-done.2 = bf16[1024,64]{0,1:T(8,128)(2,1)S(1)} copy-done((bf16[1024,64]{0,1:T(8,128)(2,1)S(1)}, bf16[1024,64]{0,1:T(8,128)(2,1)}, u32[]{:S(2)}) %copy-start.2) | copy-done | bytes 131096
  3.4 0.0 copy-start.3
  3.4 0.9 %copy-done.3 = bf16[1024,64]{0,1:T(8,128)(2,1)S(1)} copy-done((bf16[1024,64]{0,1:T(8,128)(2,1)S(1)}, bf16[1024,64]{0,1:T(8,128)(2,1)}, u32[]{:S(2)}) %copy-start.3) | copy-done | bytes 131096
  4.3 0.0 copy-start.4
  4.3 0.8 %copy-done.4 = bf16[16,1024]{1,0:T(8,128)(2,1)S(1)} copy-done((bf16[16,1024]{1,0:T(8,128)(2,1)S(1)}, bf16[16,1024]{1,0:T(8,128)(2,1)}, u32[]{:S(2)}) %copy-start.4) | copy-done | bytes 32792
  5.0 0.0 copy-start.5
  5.0 0.7 %copy-done.5 = bf16[3,1024]{1,0:T(4,128)(2,1)S(1)} copy-done((bf16[3,1024]{1,0:T(4,128)(2,1)S(1)}, bf16[3,1024]{1,0:T(4,128)(2,1)}, u32[]{:S(2)}) %copy-start.5) | copy-done | bytes 6168
  5.7 0.0 copy-start.6
  5.7 0.7 %copy-done.6 = s32[2,256]{1,0:T(2,128)S(1)} copy-done((s32[2,256]{1,0:T(2,128)S(1)}, s32[2,256]{1,0:T(2,128)}, u32[]{:S(2)}) %copy-start.6) | copy-done | bytes 2072
  6.4 0.0 copy-start.7
  6.4 0.7 %copy-done.7 = s32[2]{0:T(128)S(1)} copy-done((s32[2]{0:T(128)S(1)}, s32[2]{0:T(128)}, u32[]{:S(2)}) %copy-start.7) | copy-done | bytes 32
  7.1 43.9 %attribution.1 = f32[2,1024]{1,0:T(2,128)S(1)} custom-call(bf16[2,256,1024]{2,1,0:T(8,128)(2,1)S(1)} %copy-done, s32[2,256]{1,0:T(2,128)S(1)} %copy-done.6, s32[2]{0:T(128)S(1)} %copy-done.7, bf16[3,1024]{1,0:T(4,128)(2,1)S(1)} %copy-done.5, bf16[1024,4096]{1,0:T(8,128)(2,1)} %proj_weight.1, bf16[512,1024]{1,0:T(8,128)(2,1)S(1)} %copy-done.1, ...), custom_call_target="tpu_custom_call" | custom-call | tf_op jit(solution)/shard_map/attribution/pallas_call | solution.py:387
  51.0 0.6 %copy.11 = f32[2,1024]{1,0:T(2,128)} copy(f32[2,1024]{1,0:T(2,128)S(1)} %attribution.1) | data formatting | bytes 16384
Async XLA Ops:
  0.0 1.2 %copy-start = (bf16[2,256,1024]{2,1,0:T(8,128)(2,1)S(1)}, bf16[2,256,1024]{2,1,0:T(8,128)(2,1)}, u32[]{:S(2)}) copy-start(bf16[2,256,1024]{2,1,0:T(8,128)(2,1)} %hidden.1) | copy-start | bytes 3145732
  1.2 1.2 %copy-start.1 = (bf16[512,1024]{1,0:T(8,128)(2,1)S(1)}, bf16[512,1024]{1,0:T(8,128)(2,1)}, u32[]{:S(2)}) copy-start(bf16[512,1024]{1,0:T(8,128)(2,1)} %unembed.1) | copy-start | bytes 3145732
  2.5 0.9 %copy-start.2 = (bf16[1024,64]{0,1:T(8,128)(2,1)S(1)}, bf16[1024,64]{0,1:T(8,128)(2,1)}, u32[]{:S(2)}) copy-start(bf16[1024,64]{0,1:T(8,128)(2,1)} %param.15) | copy-start | bytes 393220
  3.4 0.9 %copy-start.3 = (bf16[1024,64]{0,1:T(8,128)(2,1)S(1)}, bf16[1024,64]{0,1:T(8,128)(2,1)}, u32[]{:S(2)}) copy-start(bf16[1024,64]{0,1:T(8,128)(2,1)} %param.16) | copy-start | bytes 393220
  4.3 0.8 %copy-start.4 = (bf16[16,1024]{1,0:T(8,128)(2,1)S(1)}, bf16[16,1024]{1,0:T(8,128)(2,1)}, u32[]{:S(2)}) copy-start(bf16[16,1024]{1,0:T(8,128)(2,1)} %queries.1) | copy-start | bytes 98308
  5.0 0.7 %copy-start.5 = (bf16[3,1024]{1,0:T(4,128)(2,1)S(1)}, bf16[3,1024]{1,0:T(4,128)(2,1)}, u32[]{:S(2)}) copy-start(bf16[3,1024]{1,0:T(4,128)(2,1)} %conv_filter.1) | copy-start | bytes 18436
  5.7 0.7 %copy-start.6 = (s32[2,256]{1,0:T(2,128)S(1)}, s32[2,256]{1,0:T(2,128)}, u32[]{:S(2)}) copy-start(s32[2,256]{1,0:T(2,128)} %targets.1) | copy-start | bytes 6148
  6.4 0.7 %copy-start.7 = (s32[2]{0:T(128)S(1)}, s32[2]{0:T(128)}, u32[]{:S(2)}) copy-start(s32[2]{0:T(128)} %lengths.1) | copy-start | bytes 28

commit v2 on v1

v2 whole, which is shorter than its diff:
```python
import jax
import jax.numpy as jnp
from jax import lax
from jax.experimental import pallas as pl
from jax.experimental.pallas import tpu as pltpu
from jax.sharding import PartitionSpec as P

EPS = 1e-06
MESH = pl.DeviceIdType.MESH
F32 = jnp.float32
BF16 = jnp.bfloat16

LOCAL = 512
WIDTH = 1024
SIDE = 64
ROWS = LOCAL + SIDE
PANELS = 2
PANEL = LOCAL // PANELS
PIECE = PANEL // 4
HALF = PIECE // 2


def nt(left, right, precision=None):
    return lax.dot_general(
        left, right, (((1,), (1,)), ((), ())), precision=precision, preferred_element_type=F32
    )


def kernel(
    hidden,
    targets_in,
    lengths_in,
    filter_in,
    proj_weight,
    unembed,
    proj_in_t,
    proj_out_t,
    queries,
    out,
    targets,
    lengths,
    conv_filter,
    held,
    mixed,
    weight,
    words,
    words_sib,
    words_far,
    side_in_w,
    side_out_w,
    folded,
    folded_low,
    up_part,
    up_sib,
    up_chip,
    up_far,
    logits_full,
    logits_low,
    from_sib,
    to_near,
    from_near,
    side_t,
    query_all,
    grad_out,
    grad_all,
    grad_rows,
    score_out,
    score_all,
    local_sem,
    uz_send,
    uz_recv,
    us_send,
    us_recv,
    uf_send,
    uf_recv,
    w_send,
    w_recv,
    up_send,
    up_recv,
    a_send,
    a_recv,
    b_send,
    b_recv,
    qz_send,
    qz_recv,
    qx_send,
    qx_recv,
    g_send,
    g_recv,
    s_send,
    s_recv,
):
    dp = lax.axis_index("dp")
    tensor = lax.axis_index("tensor")
    x, y, zh = dp // 16, (dp // 4) % 4, dp % 4
    zl, core = tensor // 2, tensor % 2
    me = y * 4 + tensor
    colours = [(x + 2 * y) % 4, (2 * x + y) % 4]
    pieces = [pl.ds(pl.multiple_of(p * PANEL + colours[p] * PIECE, PIECE), PIECE) for p in range(PANELS)]
    packed = [pl.ds(p * PIECE, PIECE) for p in range(PANELS)]
    far_dp = dp - zh + (zh + 2 * zl + 3) % 4
    sib = (dp, zl * 2 + 1 - core)
    near = (dp, (1 - zl) * 2 + core)
    far = (far_dp, (1 - zl) * 2 + core)

    def at_x(step):
        return (dp - x * 16 + ((x + step) % 4) * 16, tensor)

    def at_y(step):
        return (dp - y * 4 + ((y + step) % 4) * 4, tensor)

    def at_z(step):
        return (dp - zh + (zh + step) % 4, tensor)

    def member(place):
        return (dp - y * 4 + (place // 4) * 4, place % 4)

    def remote(src, dst, send, recv, device):
        return pltpu.make_async_remote_copy(
            src_ref=src, dst_ref=dst, send_sem=send, recv_sem=recv, device_id=device, device_id_type=MESH
        )

    barrier = pltpu.get_barrier_semaphore()
    partners = [far, sib, near, (dp, (1 - zl) * 2 + 1 - core)]
    partners += [at_x(i) for i in (1, 2, 3)] + [at_z(i) for i in (1, 2, 3)]
    partners += [member((me + 4 * turn) % 16 - tensor + (tensor + step) % 4) for turn in (1, 2, 3) for step in range(4)]
    for device in partners:
        pl.semaphore_signal(barrier, inc=1, device_id=device, device_id_type=MESH)

    slices = (tensor, zl * 2 + 1 - core, (1 - zl) * 2 + core, (1 - zl) * 2 + 1 - core)
    own_queries = query_all.at[pl.ds(pl.multiple_of(x * 64 + zh * 16, 16), 16)]

    def x_queries(step, size, first=0):
        return query_all.at[pl.ds(pl.multiple_of((x + step) % 4 * 64 + first, size), size)]

    local = [
        (hidden, held),
        (filter_in, conv_filter),
        (unembed, words),
        (proj_out_t, side_out_w),
    ]
    local += [
        (proj_weight.at[:, pl.ds(pl.multiple_of(slices[i] * WIDTH, WIDTH), WIDTH)], weight.at[i]) for i in range(4)
    ]
    local += [(proj_in_t, side_in_w), (queries, own_queries), (targets_in, targets), (lengths_in, lengths)]
    loads = [pltpu.make_async_copy(src, dst, local_sem.at[i]) for i, (src, dst) in enumerate(local)]
    for i in (2, 4, 5):
        loads[i].start()

    pl.semaphore_wait(barrier, len(partners))

    sends, word_copies, sib_copies = [], [], []
    for p in range(PANELS):
        copies = []
        for side, device in enumerate((near, far)):
            rows = pl.ds(pl.multiple_of(p * PANEL + colours[p] * PIECE + side * HALF, HALF), HALF)
            copy = remote(
                unembed.at[rows],
                words_far.at[0, pl.ds(p * PIECE + side * HALF, HALF)],
                uz_send.at[p, side],
                uz_recv.at[p, side],
                device,
            )
            copy.start()
            copies.append(copy)
        word_copies.append(copies)
        sends.extend(copies)
    for p in range(PANELS):
        copy = remote(unembed.at[pieces[p]], words_sib.at[packed[p]], us_send.at[p], us_recv.at[p], sib)
        copy.start()
        sib_copies.append(copy)
    sends.extend(sib_copies)

    for i in (6, 7, 0, 1, 3, 8, 9, 10, 11):
        loads[i].start()


    loads[2].wait()
    loads[4].wait()
    folded[...] = nt(jnp.concatenate([words[rows] for rows in pieces], axis=0), weight[0])

    a_copies, b_copies = {}, {}
    bands = [pl.ds(i * 128, 128) for i in range(4)] + [pl.ds(LOCAL, SIDE)]

    def send_a(index, part):
        rows = bands[index]
        for quarter in range(4):
            columns = part[:, quarter * 128 : (quarter + 1) * 128]
            logits_full[quarter % 2, quarter // 2, rows] = columns
            logits_low[quarter % 2, quarter // 2, rows] = columns.astype(BF16)
        copy = remote(
            logits_low.at[1 - core, :, rows], from_sib.at[:, rows], a_send.at[index], a_recv.at[index], sib
        )
        copy.start()
        a_copies[index] = copy

    def send_b(index):
        rows = bands[index]
        a_copies[index].wait_recv()
        chip = logits_full[core, 1 - zl, rows] + from_sib[1 - zl, rows].astype(F32)
        to_near[rows] = chip.astype(BF16)
        copy = remote(to_near.at[rows], from_near.at[rows], b_send.at[index], b_recv.at[index], near)
        copy.start()
        b_copies[index] = copy

    for copy in sib_copies:
        copy.wait_recv()
    loads[5].wait()
    folded[...] += nt(words_sib[...], weight[1])

    w_copies, forwards = [], []

    def arrive(p):
        for copy in word_copies[p]:
            copy.wait_recv()
        copy = remote(words_far.at[0, packed[p]], words_far.at[1, packed[p]], uf_send.at[p], uf_recv.at[p], sib)
        copy.start()
        forwards.append(copy)
        folded[packed[p]] += nt(words_far[0, packed[p]], weight[2])

    def fold(p):
        forwards[p].wait_recv()
        part = folded[packed[p]] + nt(words_far[1, packed[p]], weight[3])
        folded_low[pieces[p]] = part.astype(BF16)
        along, across = (at_x, at_y) if p == 0 else (at_y, at_x)
        copies = []
        for i, device in enumerate((along(1), along(3))):
            copies.append(
                remote(folded_low.at[pieces[p]], folded_low.at[pieces[p]], w_send.at[p, i], w_recv.at[p, i], device)
            )
        for i, device in enumerate((across(1), across(3))):
            rows = pl.ds(pl.multiple_of(p * PANEL + colours[p] * PIECE + i * HALF, HALF), HALF)
            copies.append(
                remote(folded_low.at[rows], folded_low.at[rows], w_send.at[p, 2 + i], w_recv.at[p, 2 + i], device)
            )
        for copy in copies:
            copy.start()
        w_copies.append(copies)
        sends.extend(copies)

    def logits_of(p, half):
        if half == 0:
            for copy in w_copies[p]:
                copy.wait_recv()
        index = 2 * p + half
        send_a(index, nt(folded_low[bands[index]], mixed[...]))

    loads[6].wait()
    arrive(0)
    arrive(1)

    loads[7].wait()
    fold(0)
    fold(1)
    sends.extend(forwards)

    loads[9].wait()
    qz_copies = []
    for step in (1, 2, 3):
        copy = remote(queries, own_queries, qz_send.at[step], qz_recv.at[step], at_z(step))
        copy.start()
        qz_copies.append(copy)

    loads[0].wait()
    loads[1].wait()
    chunk = 256
    first_row = lax.broadcasted_iota(jnp.int32, (256, chunk), 0)

    def convolve(i, carry):
        row = i // (WIDTH // chunk)
        columns = pl.ds(pl.multiple_of((i % (WIDTH // chunk)) * chunk, chunk), chunk)
        values = held[row, :, columns].astype(F32)
        taps = conv_filter[:, columns].astype(F32)
        first = jnp.where(first_row < 1, 0.0, pltpu.roll(values, 1, 0))
        second = jnp.where(first_row < 2, 0.0, pltpu.roll(values, 2, 0))
        result = taps[0:1] * values + taps[1:2] * first + taps[2:3] * second
        mixed[pl.ds(pl.multiple_of(row * 256, 256), 256), columns] = result.astype(BF16)
        return carry

    lax.fori_loop(0, 2 * (WIDTH // chunk), convolve, 0)

    loads[3].wait()
    up_part[...] = nt(side_out_w[...], words[...])
    up_to_sib = remote(up_part, up_sib, up_send.at[0], up_recv.at[0], sib)
    up_to_sib.start()
    sends.append(up_to_sib)

    loads[8].wait()
    send_a(4, nt(side_in_w[...], mixed[...]))

    up_to_sib.wait_recv()
    up_chip[...] = up_part[...] + up_sib[...]
    up_copies = []
    for side, device in enumerate((near, far)):
        rows = pl.ds(side * (SIDE // 2), SIDE // 2)
        copy = remote(up_chip.at[rows], up_far.at[rows], up_send.at[1 + side], up_recv.at[1 + side], device)
        copy.start()
        up_copies.append(copy)
    sends.extend(up_copies)
    send_b(4)

    logits_of(0, 0)
    logits_of(0, 1)
    for copy in qz_copies:
        copy.wait_recv()
    qx_copies = []
    for step in (1, 3):
        copy = remote(x_queries(0, 64), x_queries(0, 64), qx_send.at[step], qx_recv.at[step], at_x(step))
        copy.start()
        qx_copies.append(copy)
    logits_of(1, 0)
    send_b(0)
    logits_of(1, 1)
    send_b(1)
    send_b(2)
    send_b(3)
    for copy in qx_copies:
        copy.wait_recv()
    for i, (step, source, first) in enumerate(((1, 3, 0), (3, 1, 32))):
        rows = x_queries(source, 32, first)
        copy = remote(rows, rows, qx_send.at[2 * i], qx_recv.at[2 * i], at_x(step))
        copy.start()
        qx_copies.append(copy)
    sends.extend(qz_copies + qx_copies)
    sends.extend(list(a_copies.values()) + list(b_copies.values()))

    for copy in up_copies:
        copy.wait_recv()
    up = (up_chip[...] + up_far[...]).astype(BF16)
    for copy in b_copies.values():
        copy.wait_recv()
    total = logits_full[core, zl] + from_sib[zl].astype(F32) + from_near[...].astype(F32)
    expo = jnp.exp(total[:LOCAL])
    prob = expo / jnp.sum(expo, axis=0, keepdims=True)
    loads[10].wait()
    loads[11].wait()
    position = lax.broadcasted_iota(jnp.int32, (1, 128), 1) + core * 128
    live = (position < lengths[zl]).astype(F32)
    ids = [jnp.where(zl == 0, targets[0:1, i : i + 128], targets[1:2, i : i + 128]) for i in (0, 128)]
    target = jnp.where(core == 0, ids[0], ids[1])
    onehot = (lax.broadcasted_iota(jnp.int32, (LOCAL, 128), 0) == target).astype(F32)
    grad_logits = ((prob - onehot) * live).astype(BF16)
    side_out = jnp.dot(up, grad_logits, preferred_element_type=F32)
    side_t[...] = total[LOCAL:]
    even = nt(side_t[pl.ds(0, SIDE // 2, stride=2), :], side_out, lax.Precision.HIGHEST)
    odd = nt(side_t[pl.ds(1, SIDE // 2, stride=2), :], side_out, lax.Precision.HIGHEST)
    row_grad = jnp.concatenate([even, odd], axis=1)
    for share in range(4):
        grad_out[share] = row_grad[share * 8 : (share + 1) * 8]

    order = [(me + 4 * turn) % 16 - tensor + (tensor + step) % 4 for turn in (2, 1, 3) for step in range(4)]
    order += [me - tensor + (tensor + step) % 4 for step in (1, 2, 3)]
    tail = grad_all.at[pl.ds(0, 15)]

    grad_all[me] = grad_out[tensor]
    grad_copies = []
    for place in order:
        copy = remote(grad_out.at[place % 4], grad_all.at[me], g_send, g_recv, member(place))
        copy.start()
        grad_copies.append(copy)
    for copy in qx_copies[2:]:
        copy.wait_recv()
    pltpu.make_async_copy(tail, tail, g_recv).wait()

    norms = []
    for row in range(8):
        whole = grad_all[2 * row] + grad_all[2 * row + 1]
        grad_rows[pl.ds(row * 8, 8)] = whole
        norms.append(jnp.sum(whole * whole, axis=(0, 1), keepdims=True))
    flat = jnp.concatenate([grad_rows[pl.ds(i, 8, stride=8), :] for i in range(8)], axis=1).astype(BF16)
    scores = nt(flat, query_all[...])
    for row in range(8):
        for half in range(2):
            score_out[row // 2, pl.ds((row % 2) * 2 + half, 1)] = scores[
                row : row + 1, half * 128 : (half + 1) * 128
            ]
            score_out[row // 2, pl.ds(4 + (row % 2) * 2 + half, 1)] = jnp.broadcast_to(norms[row], (1, 128))

    score_all[me] = score_out[y]
    score_copies = []
    for place in order:
        copy = remote(score_out.at[place // 4], score_all.at[me], s_send, s_recv, member(place))
        copy.start()
        score_copies.append(copy)
    pltpu.make_async_copy(tail, tail, s_recv).wait()

    sums = [score_all[4 * i] + score_all[4 * i + 1] + score_all[4 * i + 2] + score_all[4 * i + 3] for i in range(4)]
    scale = jnp.sqrt(sums[0][4:8] + EPS)
    low_lanes = lax.broadcasted_iota(jnp.int32, (8, 128), 1) < 64
    turned = [pltpu.roll(part, 64, 1) for part in sums]
    for odd_x in range(2):
        for pair in range(2):
            left = (turned if odd_x else sums)[2 * pair]
            right = (sums if odd_x else turned)[2 * pair + 1]
            line = jnp.where(low_lanes, left, right)[0:4] / scale
            for row in range(2):
                for half in range(2):
                    column = 128 * (4 * half + 2 * odd_x + pair)
                    out[pl.ds(row, 1), pl.ds(column, 128)] = line[2 * row + half : 2 * row + half + 1]

    for sem in (g_send, s_send):
        pltpu.make_async_copy(tail, tail, sem).wait()
    for copy in sends:
        copy.wait_send()


def per_device(hidden, targets, lengths, conv_filter, proj_weight, unembed, proj_in, proj_out, query_grads):
    hbm = pl.BlockSpec(memory_space=pltpu.HBM)
    vmem = pl.BlockSpec(memory_space=pltpu.VMEM)
    dma = pltpu.SemaphoreType.DMA
    scratch = [
        pltpu.VMEM((2, 256), jnp.int32),
        pltpu.SMEM((2,), jnp.int32),
        pltpu.VMEM((3, WIDTH), BF16),
        pltpu.VMEM((2, 256, WIDTH), BF16),
        pltpu.VMEM((LOCAL, WIDTH), BF16),
        pltpu.VMEM((4, WIDTH, WIDTH), BF16),
        pltpu.VMEM((LOCAL, WIDTH), BF16),
        pltpu.VMEM((PANELS * PIECE, WIDTH), BF16),
        pltpu.VMEM((2, PANELS * PIECE, WIDTH), BF16),
        pltpu.VMEM((SIDE, WIDTH), BF16),
        pltpu.VMEM((SIDE, WIDTH), BF16),
        pltpu.VMEM((PANELS * PIECE, WIDTH), F32),
        pltpu.VMEM((LOCAL, WIDTH), BF16),
        pltpu.VMEM((SIDE, LOCAL), F32),
        pltpu.VMEM((SIDE, LOCAL), F32),
        pltpu.VMEM((SIDE, LOCAL), F32),
        pltpu.VMEM((SIDE, LOCAL), F32),
        pltpu.VMEM((2, 2, ROWS, 128), F32),
        pltpu.VMEM((2, 2, ROWS, 128), BF16),
        pltpu.VMEM((2, ROWS, 128), BF16),
        pltpu.VMEM((ROWS, 128), BF16),
        pltpu.VMEM((ROWS, 128), BF16),
        pltpu.VMEM((SIDE, 128), F32),
        pltpu.VMEM((256, WIDTH), BF16),
        pltpu.VMEM((4, 8, 128), F32),
        pltpu.VMEM((16, 8, 128), F32),
        pltpu.VMEM((64, 128), F32),
        pltpu.VMEM((4, 8, 128), F32),
        pltpu.VMEM((16, 8, 128), F32),
        dma((12,)),
        dma((PANELS, 2)),
        dma((PANELS, 2)),
        dma((PANELS,)),
        dma((PANELS,)),
        dma((PANELS,)),
        dma((PANELS,)),
        dma((PANELS, 4)),
        dma((PANELS, 4)),
        dma((3,)),
        dma((3,)),
        dma((5,)),
        dma((5,)),
        dma((5,)),
        dma((5,)),
        dma((4,)),
        dma((4,)),
        dma((4,)),
        dma((4,)),
        dma,
        dma,
        dma,
        dma,
    ]
    return pl.pallas_call(
        kernel,
        out_shape=jax.ShapeDtypeStruct((2, 1024), F32),
        in_specs=[hbm] * 9,
        out_specs=vmem,
        scratch_shapes=scratch,
        compiler_params=pltpu.CompilerParams(
            collective_id=0, has_side_effects=True, vmem_limit_bytes=64 * 1024 * 1024
        ),
        name="attribution",
    )(hidden, targets, lengths, conv_filter, proj_weight, unembed, proj_in.T, proj_out.T, query_grads)


def solution(mesh):
    in_specs = (
        P("dp", None, "tensor"),
        P("dp", None),
        P("dp"),
        P(None, "tensor"),
        P("tensor", None),
        P(None, "tensor"),
        P("tensor", None),
        P("tensor", None),
        P("dp", "tensor"),
    )
    return jax.shard_map(
        per_device, mesh=mesh, in_specs=in_specs, out_specs=P("dp", None), check_vma=False
    )
```

time: 51.9 us -> 40.8 us (0.79)
  local copies, waits for them, and re-layouts: 7.65 us -> 1.3 us
  Pallas kernels: 43.9 us -> 39.3 us
    unnamed x17 -> x1, local copies, waits for them, and re-layouts: 7.65 us -> 1.3 us
    pallas_call x1, Pallas kernels: 43.9 us -> 39.3 us  [per_device(): pl.pallas_call(kernel, out_shape=jax.ShapeDtypeStruct((2, 1024), F32), in...]
where the time goes in v2:
time: 40.8 us; the launch traced here: 40.6 us
  Pallas kernels  39.3 us (96%)
  local copies, waits for them, and re-layouts  1.3 us (3%)
    pallas_call x1, Pallas kernels, per_device(): pl.pallas_call(kernel, out_shape=jax.ShapeDtypeStruct((2, 1024), F32), in...  39.3 us
    unnamed x1, local copies, waits for them, and re-layouts  1.3 us

profile of v2, /device:TPU:1, one launch (start us, length us, event | category | flops | bytes accessed | tf_op | source)
XLA Modules:
  0.0 40.6 jit_solution(6139701814125889790)
XLA Ops:
  0.0 39.3 %attribution.1 = f32[2,1024]{1,0:T(2,128)} custom-call(bf16[2,256,1024]{2,1,0:T(8,128)(2,1)} %hidden.1, s32[2,256]{1,0:T(2,128)} %targets_in.1, s32[2]{0:T(128)} %lengths_in.1, bf16[3,1024]{1,0:T(4,128)(2,1)} %filter_in.1, bf16[1024,4096]{1,0:T(8,128)(2,1)} %proj_weight.1, bf16[512,1024]{1,0:T(8,128)(2,1)} %unembed.1, bf16[64,1024]{1,0:T(8,128)(2,1)} %bitcast.2, ...), custom_call_target="tpu_custom_call" | custom-call | tf_op jit(solution)/shard_map/attribution/pallas_call | solution.py:465
  39.3 1.3 %copy.11 = f32[2,1024]{1,0:T(2,128)} copy(f32[2,1024]{1,0:T(2,128)} %attribution.1) | data formatting | bytes 16384

commit v3 on v2

--- a/solution.py
+++ b/solution.py
@@ -121,9 +121,9 @@
         )
 
     barrier = pltpu.get_barrier_semaphore()
-    partners = [far, sib, near, (dp, (1 - zl) * 2 + 1 - core)]
-    partners += [at_x(i) for i in (1, 2, 3)] + [at_z(i) for i in (1, 2, 3)]
-    partners += [member((me + 4 * turn) % 16 - tensor + (tensor + step) % 4) for turn in (1, 2, 3) for step in range(4)]
+    partners = [at_z(2), at_z(1), at_z(3)]
+    partners += [member((me + 4 * turn) % 16 - tensor + (tensor + step) % 4) for turn in (2, 1, 3) for step in range(4)]
+    partners += [at_x(1), at_x(3), far, (dp, (1 - zl) * 2 + 1 - core), near, sib]
     for device in partners:
         pl.semaphore_signal(barrier, inc=1, device_id=device, device_id_type=MESH)
 
@@ -180,7 +180,7 @@
     folded[...] = nt(jnp.concatenate([words[rows] for rows in pieces], axis=0), weight[0])
 
     a_copies, b_copies = {}, {}
-    bands = [pl.ds(i * 128, 128) for i in range(4)] + [pl.ds(LOCAL, SIDE)]
+    bands = [pl.ds(p * PANEL, PANEL) for p in range(PANELS)] + [pl.ds(LOCAL, SIDE)]
 
     def send_a(index, part):
         rows = bands[index]
@@ -238,15 +238,21 @@
         w_copies.append(copies)
         sends.extend(copies)
 
-    def logits_of(p, half):
-        if half == 0:
-            for copy in w_copies[p]:
-                copy.wait_recv()
-        index = 2 * p + half
-        send_a(index, nt(folded_low[bands[index]], mixed[...]))
+    def logits_of(p):
+        for copy in w_copies[p]:
+            copy.wait_recv()
+        send_a(p, nt(folded_low[bands[p]], mixed[...]))
 
     loads[6].wait()
     arrive(0)
+
+    loads[9].wait()
+    qz_copies = []
+    for step in (1, 2, 3):
+        copy = remote(queries, own_queries, qz_send.at[step], qz_recv.at[step], at_z(step))
+        copy.start()
+        qz_copies.append(copy)
+
     arrive(1)
 
     loads[7].wait()
@@ -254,12 +260,11 @@
     fold(1)
     sends.extend(forwards)
 
-    loads[9].wait()
-    qz_copies = []
-    for step in (1, 2, 3):
-        copy = remote(queries, own_queries, qz_send.at[step], qz_recv.at[step], at_z(step))
-        copy.start()
-        qz_copies.append(copy)
+    loads[3].wait()
+    up_part[...] = nt(side_out_w[...], words[...])
+    up_to_sib = remote(up_part, up_sib, up_send.at[0], up_recv.at[0], sib)
+    up_to_sib.start()
+    sends.append(up_to_sib)
 
     loads[0].wait()
     loads[1].wait()
@@ -279,14 +284,8 @@
 
     lax.fori_loop(0, 2 * (WIDTH // chunk), convolve, 0)
 
-    loads[3].wait()
-    up_part[...] = nt(side_out_w[...], words[...])
-    up_to_sib = remote(up_part, up_sib, up_send.at[0], up_recv.at[0], sib)
-    up_to_sib.start()
-    sends.append(up_to_sib)
-
     loads[8].wait()
-    send_a(4, nt(side_in_w[...], mixed[...]))
+    send_a(2, nt(side_in_w[...], mixed[...]))
 
     up_to_sib.wait_recv()
     up_chip[...] = up_part[...] + up_sib[...]
@@ -297,10 +296,9 @@
         copy.start()
         up_copies.append(copy)
     sends.extend(up_copies)
-    send_b(4)
-
-    logits_of(0, 0)
-    logits_of(0, 1)
+
+    logits_of(0)
+    send_b(2)
     for copy in qz_copies:
         copy.wait_recv()
     qx_copies = []
@@ -308,12 +306,9 @@
         copy = remote(x_queries(0, 64), x_queries(0, 64), qx_send.at[step], qx_recv.at[step], at_x(step))
         copy.start()
         qx_copies.append(copy)
-    logits_of(1, 0)
+    logits_of(1)
     send_b(0)
-    logits_of(1, 1)
     send_b(1)
-    send_b(2)
-    send_b(3)
     for copy in qx_copies:
         copy.wait_recv()
     for i, (step, source, first) in enumerate(((1, 3, 0), (3, 1, 32))):
@@ -449,10 +444,10 @@
         dma((PANELS, 4)),
         dma((3,)),
         dma((3,)),
-        dma((5,)),
-        dma((5,)),
-        dma((5,)),
-        dma((5,)),
+        dma((3,)),
+        dma((3,)),
+        dma((3,)),
+        dma((3,)),
         dma((4,)),
         dma((4,)),
         dma((4,)),

time: 40.8 us -> 40.6 us (level)
  no operation moved by 1% of the time
where the time goes in v3:
time: 40.6 us; the launch traced here: 40.5 us
  Pallas kernels  39.2 us (97%)
  local copies, waits for them, and re-layouts  1.3 us (3%)
    pallas_call x1, Pallas kernels, per_device(): pl.pallas_call(kernel, out_shape=jax.ShapeDtypeStruct((2, 1024), F32), in...  39.2 us
    unnamed x1, local copies, waits for them, and re-layouts  1.3 us

profile of v3, /device:TPU:1, one launch (start us, length us, event | category | flops | bytes accessed | tf_op | source)
XLA Modules:
  0.0 40.5 jit_solution(3888914719199491869)
XLA Ops:
  0.0 39.2 %attribution.1 = f32[2,1024]{1,0:T(2,128)} custom-call(bf16[2,256,1024]{2,1,0:T(8,128)(2,1)} %hidden.1, s32[2,256]{1,0:T(2,128)} %targets_in.1, s32[2]{0:T(128)} %lengths_in.1, bf16[3,1024]{1,0:T(4,128)(2,1)} %filter_in.1, bf16[1024,4096]{1,0:T(8,128)(2,1)} %proj_weight.1, bf16[512,1024]{1,0:T(8,128)(2,1)} %unembed.1, bf16[64,1024]{1,0:T(8,128)(2,1)} %bitcast.2, ...), custom_call_target="tpu_custom_call" | custom-call | tf_op jit(solution)/shard_map/attribution/pallas_call | solution.py:460
  39.2 1.3 %copy.11 = f32[2,1024]{1,0:T(2,128)} copy(f32[2,1024]{1,0:T(2,128)} %attribution.1) | data formatting | bytes 16384
